TPU v7x, 32 devices: a whole 2x2x4 slice. The times are simulated.
32 devices in a mesh: orb: 8 (over z, core), bas: 4 (over y, x).
Axes of the slice: x: 2, y: 2, z: 4, core: 2. Of those that a mesh axis runs over, the one named last changes fastest.
Arguments:
- coeffs: bfloat16 [131072, 1024], P('bas', 'orb'), may hold values from -6 to 6
- dipole: bfloat16 [3, 4, 32768, 384], P(None, 'bas', 'orb'), may hold values from -0.0008544922 to 0.0008544922
- tile_cols: int32 [4, 256, 3], P('bas', 'orb'), may hold values from -1 to 31, as said below
- matching: int32 [1, 8], replicated, may hold values from 0 to 7, as said below
Outputs:
- localized: bfloat16 [131072, 1024], P('bas', 'orb')
Inputs may be any that keep to these rules, and one draw needn't show every extreme that they name: `tile_cols`: entry [b, r, s] is the column tile of slot s of row tile r of basis block b, counted within the row tile's group of 32 tiles, or -1 for a padded slot; slot 0 is the row tile itself, and the live slots of a row name distinct tiles. `matching`: each row pairs every block with another block and is its own inverse; the rows are distinct rounds of one round-robin tournament.
All inputs are finite; a program needn't handle non-finite values.
Results may differ from a plain program's by a relative error of at most 0.0047.
Values may be sent and summed in bfloat16 or wider, within the bound.
A program may use at most 192 MiB of HBM per device.

v0:
```python
import jax
import jax.numpy as jnp
from jax import lax
from jax.sharding import PartitionSpec as P

BLK = 128
TILE = 128
SLOTS = 3
SWEEPS = 4


def jacobi_pair(gram):
    highest = lax.Precision.HIGHEST
    half = gram.shape[1] // 2
    positions = jnp.arange(half, dtype=jnp.int32)
    accum = jnp.eye(2 * half, dtype=jnp.float32)
    for sweep_index in range(SWEEPS):
        permute = jnp.equal(positions[None, :], (positions[:, None] + sweep_index) % half).astype(
            jnp.float32
        )
        diag_vals = jnp.diagonal(gram, axis1=1, axis2=2)
        head_vals = diag_vals[:, :half]
        tail_vals = jnp.roll(diag_vals[:, half:], -sweep_index, axis=1)
        off_vals = jnp.diagonal(
            jnp.roll(gram[:, :half, half:], -sweep_index, axis=2), axis1=1, axis2=2
        )
        spread = head_vals - tail_vals
        quad_term = jnp.sum(off_vals * off_vals - 0.25 * spread * spread, axis=0)
        lin_term = jnp.sum(off_vals * spread, axis=0)
        angles = 0.25 * jnp.arctan(lin_term / (jnp.abs(quad_term) + 1.0))
        cosine = jnp.cos(angles)
        sine_part = jnp.sin(angles)
        upper_half = jnp.concatenate([jnp.diag(cosine), -(sine_part[:, None] * permute)], axis=1)
        bottom = jnp.concatenate(
            [permute.T * sine_part[None, :], jnp.diag(jnp.roll(cosine, sweep_index))], axis=1
        )
        rotation = jnp.concatenate([upper_half, bottom], axis=0)
        gram = jnp.einsum(
            "ji,kjl->kil",
            rotation,
            jnp.einsum("kij,jl->kil", gram, rotation, precision=highest),
            precision=highest,
        )
        accum = jnp.dot(accum, rotation, precision=highest)
    return accum


def project_rows(dipole_rows, tile_index, local_rows, blocks):
    group_tiles = tile_index.shape[0]
    tile_rows = local_rows.reshape(group_tiles, TILE, blocks * BLK)
    picked = tile_rows[jnp.maximum(tile_index, 0)]
    picked = jnp.where((tile_index >= 0)[:, :, None, None], picked, jnp.zeros_like(picked))
    picked = picked.reshape(group_tiles, SLOTS * TILE, blocks * BLK)
    moments = jnp.einsum(
        "kraj,rjn->kran", dipole_rows, picked, preferred_element_type=jnp.float32
    ).astype(jnp.bfloat16)
    return moments.reshape(3, group_tiles * TILE, blocks, BLK)


def gram_terms(coef_blocks, moment_blocks, partner, leader, follower):
    raw_gram = jnp.einsum(
        "rbi,krbj->bkij", coef_blocks, moment_blocks, preferred_element_type=jnp.float32
    )
    self_gram = 0.5 * (raw_gram + jnp.swapaxes(raw_gram, 2, 3))
    toward = jnp.einsum(
        "rbi,krbj->bkij",
        coef_blocks,
        moment_blocks[:, :, partner],
        preferred_element_type=jnp.float32,
    )
    cross_gram = 0.5 * (toward[leader] + jnp.swapaxes(toward[follower], 2, 3))
    return (self_gram, cross_gram)


def body(coeffs, dipole, tile_cols, matching):
    local_rows = lax.all_to_all(coeffs, "orb", split_axis=0, concat_axis=1, tiled=True)
    blocks = lax.axis_size("orb")
    my_block = lax.axis_index("orb")
    row_count = local_rows.shape[0]
    dipole_rows = dipole[:, 0].reshape(3, tile_cols.shape[1], TILE, SLOTS * TILE)
    tile_index = tile_cols[0]
    block_ids = jnp.arange(blocks, dtype=jnp.int32)
    partner = matching[0]
    leader = jnp.minimum(block_ids, partner)
    follower = jnp.maximum(block_ids, partner)
    moments = project_rows(dipole_rows, tile_index, local_rows, blocks)
    coef_blocks = local_rows.reshape(row_count, blocks, BLK)
    self_gram, cross_gram = gram_terms(coef_blocks, moments, partner, leader, follower)
    my_leader = leader[my_block]
    entries = jnp.stack([self_gram[leader], self_gram[follower], cross_gram], axis=1)
    summed = lax.psum_scatter(entries, "orb", scatter_dimension=0, tiled=True)[0]
    summed = lax.psum(summed, "bas")
    lead_gram = summed[0]
    follow_gram = summed[1]
    cross_mine = summed[2]
    upper_half = jnp.concatenate([lead_gram, cross_mine], axis=2)
    lower_half = jnp.concatenate([jnp.swapaxes(cross_mine, 1, 2), follow_gram], axis=2)
    rotor = jacobi_pair(jnp.concatenate([upper_half, lower_half], axis=1))
    weight = jnp.where(my_leader == my_block, rotor[:, :BLK], rotor[:, BLK:]).astype(jnp.bfloat16)
    weights = lax.all_gather(weight[None], "orb", axis=0, tiled=True)
    is_lead = (leader == block_ids)[:, None, None]
    self_weight = jnp.where(is_lead, weights[:, :BLK], weights[:, BLK:])
    other_weight = jnp.where(is_lead, weights[:, BLK:], weights[:, :BLK])
    rotated = jnp.einsum(
        "rbj,bjn->rbn", coef_blocks, self_weight, preferred_element_type=jnp.float32
    )
    rotated = rotated + jnp.einsum(
        "rbj,bjn->rbn", coef_blocks[:, partner], other_weight, preferred_element_type=jnp.float32
    )
    local_rows = rotated.astype(jnp.bfloat16).reshape(row_count, blocks * BLK)
    return lax.all_to_all(local_rows, "orb", split_axis=1, concat_axis=0, tiled=True)


def solution(mesh):
    in_specs = (P("bas", "orb"), P(None, "bas", "orb", None), P("bas", "orb", None), P())
    out_specs = P("bas", "orb")
    return jax.shard_map(body, mesh=mesh, in_specs=in_specs, out_specs=out_specs, check_vma=False)
```

profile of v0, /device:TPU:0, one launch (start us, length us, event | category | flops | bytes accessed | tf_op | source)
XLA Modules:
  0.0 982.3 jit_solution(16487530379932482928)
XLA Ops:
  14.1 182.9 %all-to-all-done = bf16[8,4096,128]{2,1,0:T(8,128)(2,1)} async-done(((bf16[8,4096,128]{2,1,0:T(8,128)(2,1)}), bf16[8,4096,128]{2,1,0:T(8,128)(2,1)}, u32[]{:S(2)}, u32[]{:S(2)}) %all-to-all-start) | async-done | bytes 8388640 | tf_op jit(solution)/shard_map/all_to_all | solution.py:76
  207.3 13.3 %reshape.298 = bf16[32,128,1024]{2,1,0:T(8,128)(2,1)} reshape(bf16[4096,8,128]{2,1,0:T(8,128)(2,1)} %copy.135) | data formatting | bytes 16777216 | tf_op jit(solution)/shard_map/reshape | solution.py:50
  220.6 13.6 %gather_fusion = bf16[96,128,1024]{2,1,0:T(8,128)(2,1)} fusion(bf16[32,128,1024]{2,1,0:T(8,128)(2,1)} %reshape.298, s32[1024]{0:T(1024)S(1)} %pad_clamp_fusion.3), kind=kCustom, calls=%fused_computation | custom fusion | bytes 50332032 | tf_op jit(solution)/shard_map/gather | solution.py:51
  234.2 20.9 %bitcast_select_fusion = bf16[32,384,1024]{2,1,0:T(8,128)(2,1)} fusion(pred[32,384]{1,0:T(8,128)(4,1)S(1)} %bitcast.185, bf16[32,384,1024]{2,1,0:T(8,128)(2,1)} %bitcast.176), kind=kLoop, calls=%fused_computation.22 | loop fusion | flops 12582912 | bytes 50343936 | tf_op jit(solution)/shard_map/jit(_where)/select_n | solution.py:52
  255.1 25.8 %convert_bitcast_fusion = bf16[3,32,128,1024]{2,3,0,1:T(8,128)(2,1)} fusion(bf16[32,384,1024]{2,1,0:T(8,128)(2,1)} %bitcast_select_fusion, bf16[3,32,128,384]{3,2,1,0:T(8,128)(2,1)} %bitcast.200), kind=kOutput, calls=%fused_computation.23 | convolution fusion | flops 9676259328 | bytes 59768832 | tf_op jit(solution)/shard_map/kraj,rjn->kran/dot_general | solution.py:54
  281.0 32.6 %copy.139 = bf16[3,32,128,1024]{3,2,1,0:T(8,128)(2,1)} copy(bf16[3,32,128,1024]{2,3,0,1:T(8,128)(2,1)} %convert_bitcast_fusion) | data formatting | bytes 50331648 | tf_op jit(solution)/shard_map/convert_element_type | solution.py:56
  313.5 23.2 %copy.185 = bf16[1536,8,8,128]{3,2,1,0:T(8,128)(2,1)} copy(bf16[1536,8,8,128]{3,1,2,0:T(8,128)(2,1)} %bitcast.174) | data formatting | bytes 50331648
  336.7 31.7 %copy.140 = bf16[3,4096,8,128]{1,3,0,2:T(8,128)(2,1)} copy(bf16[3,4096,8,128]{3,2,1,0:T(8,128)(2,1)} %bitcast.175) | data formatting | bytes 50331648 | tf_op jit(solution)/shard_map/reshape | solution.py:57
  368.4 17.8 %fusion.95 = (bf16[3,2048,8,128]{1,3,0,2:T(8,128)(2,1)}, bf16[3,2048,8,128]{1,3,0,2:T(8,128)(2,1)}) fusion(bf16[3,4096,8,128]{1,3,0,2:T(8,128)(2,1)} %copy.140), kind=kLoop, calls=%fused_computation.191 | loop fusion | bytes 50331648 | tf_op jit(solution)/shard_map/gather | solution.py:68
  386.2 10.9 %gather_fusion.14 = bf16[8,3,2048,128]{2,3,1,0:T(8,128)(2,1)} fusion(bf16[3,2048,8,128]{1,3,0,2:T(8,128)(2,1)} %get-tuple-element.21, s32[1024]{0:T(1024)S(1)} %get-tuple-element.40), kind=kCustom, calls=%fused_computation.14 | custom fusion | bytes 25165856 | tf_op jit(solution)/shard_map/gather | solution.py:68
  397.1 10.9 %gather_fusion.15 = bf16[8,3,2048,128]{2,3,1,0:T(8,128)(2,1)} fusion(bf16[3,2048,8,128]{1,3,0,2:T(8,128)(2,1)} %get-tuple-element.22, s32[1024]{0:T(1024)S(1)} %get-tuple-element.40), kind=kCustom, calls=%fused_computation.15 | custom fusion | bytes 25165856 | tf_op jit(solution)/shard_map/gather | solution.py:68
  408.0 14.5 %fusion.19 = f32[8,3,128,128]{2,3,1,0:T(8,128)S(1)} fusion(bf16[8,4096,128]{2,1,0:T(8,128)(2,1)} %all-to-all-done, bf16[3,2048,8,128]{1,3,0,2:T(8,128)(2,1)} %bitcast.179, bf16[3,2048,8,128]{1,3,0,2:T(8,128)(2,1)} %bitcast.178), kind=kOutput, calls=%fused_computation.37 | convolution fusion | flops 3271557120 | bytes 35127296 | tf_op jit(solution)/shard_map/rbi,krbj->bkij/dot_general | solution.py:65
  426.0 14.0 %fusion.11 = f32[8,3,128,128]{3,2,1,0:T(8,128)S(1)} fusion(bf16[3,4096,8,128]{1,3,0,2:T(8,128)(2,1)} %copy.140, bf16[8,4096,128]{2,1,0:T(8,128)(2,1)} %all-to-all-done), kind=kOutput, calls=%fused_computation.28 | convolution fusion | flops 3221225472 | bytes 35127296 | tf_op jit(solution)/shard_map/rbi,krbj->bkij/dot_general | solution.py:61
  454.7 104.7 %all-reduce.6.cloned.1.call-done = f32[8,3,3,128,128]{4,3,2,0,1:T(8,128)} async-done(((f32[8,3,3,128,128]{4,3,2,0,1:T(8,128)}), f32[8,3,3,128,128]{4,3,2,0,1:T(8,128)}) %all-reduce.6.cloned.1.call-update) | async-done | bytes 4718608
  571.6 37.0 %all-reduce.4.cloned.1.call-done = f32[3,3,128,128]{3,2,1,0:T(8,128)} async-done(((f32[3,3,128,128]{3,2,1,0:T(8,128)}), f32[3,3,128,128]{3,2,1,0:T(8,128)}) %all-reduce.4.cloned.1.call-update) | async-done | bytes 589840 | tf_op jit(solution)/shard_map/psum | solution.py:92
  616.6 16.9 %copy.148 = f32[3,256,256]{0,2,1:T(8,128)} copy(f32[3,256,256]{2,1,0:T(8,128)S(1)} %maximum_maximum_fusion) | data formatting | bytes 1572864 | tf_op jit(solution)/shard_map/concatenate | solution.py:98
  638.2 16.7 %copy.153 = f32[3,256,256]{0,2,1:T(8,128)} copy(f32[3,256,256]{1,2,0:T(8,128)S(1)} %convolution_bitcast_fusion.2) | data formatting | bytes 1572864 | tf_op jit(solution)/shard_map/ji,kjl->kil/transpose | solution.py:38
  670.4 16.9 %copy.159 = f32[3,256,256]{0,2,1:T(8,128)} copy(f32[3,256,256]{1,2,0:T(8,128)S(1)} %convolution_bitcast_fusion.1) | data formatting | bytes 1572864 | tf_op jit(solution)/shard_map/ji,kjl->kil/transpose | solution.py:38
  701.8 16.7 %copy.165 = f32[3,256,256]{0,2,1:T(8,128)} copy(f32[3,256,256]{1,2,0:T(8,128)S(1)} %convolution_bitcast_fusion) | data formatting | bytes 1572864 | tf_op jit(solution)/shard_map/ji,kjl->kil/transpose | solution.py:38
  732.3 15.0 %all-gather = bf16[2048,128]{1,0:T(8,128)(2,1)S(1)} all-gather(bf16[256,128]{1,0:T(8,128)(2,1)S(1)} %fusion.47), channel_id=2, replica_groups=mesh['orb'=8,'bas'=4] {'orb'}, dimensions={0}, use_global_device_ids=true | all-gather | bytes 589824 | tf_op jit(solution)/shard_map/all_gather | solution.py:100
  747.7 11.5 %fusion.42 = f32[8,128,4096]{2,1,0:T(8,128)} fusion(bf16[8,128,128]{1,2,0:T(8,128)(2,1)S(1)} %copy.182, bf16[8,128,128]{1,2,0:T(8,128)(2,1)S(1)} %copy.183, pred[8]{0:T(512)(128)(4,1)S(1)} %iota_compare_fusion.11, bf16[8,4096,128]{2,1,0:T(8,128)(2,1)} %all-to-all-done), kind=kOutput, calls=%fused_computation.64 | convolution fusion | flops 1073872896 | bytes 25690120 | tf_op jit(solution)/shard_map/rbj,bjn->rbn/dot_general | solution.py:104
  759.2 14.0 %fusion.13 = bf16[4096,8,128]{0,2,1:T(8,128)(2,1)} fusion(f32[8,128,4096]{2,1,0:T(8,128)} %fusion.42, bf16[8,4096,128]{2,1,0:T(8,128)(2,1)} %gather_fusion.13, bf16[8,128,128]{1,2,0:T(8,128)(2,1)S(1)} %copy.183, bf16[8,128,128]{1,2,0:T(8,128)(2,1)S(1)} %copy.182, pred[8]{0:T(512)(128)(4,1)S(1)} %iota_compare_fusion.11), kind=kOutput, calls=%fused_computation.30 | convolution fusion | flops 1082261504 | bytes 34078728 | tf_op jit(solution)/shard_map/rbj,bjn->rbn/dot_general | solution.py:107
  773.3 189.9 %all_to_all.32 = bf16[4096,8,128]{0,2,1:T(8,128)(2,1)} all-to-all(bf16[4096,8,128]{0,2,1:T(8,128)(2,1)} %fusion.13), channel_id=1, replica_groups=mesh['orb'=8,'bas'=4] {'orb'}, dimensions={1} | all-to-all | bytes 16777216 | tf_op jit(solution)/shard_map/all_to_all | solution.py:111
  963.1 11.9 %copy.169 = bf16[8,4096,128]{2,1,0:T(8,128)(2,1)} copy(bf16[8,4096,128]{1,2,0:T(8,128)(2,1)} %bitcast.177) | data formatting | bytes 16777216 | tf_op jit(solution)/shard_map/all_to_all | solution.py:111
  (129 shorter events, 104.0 us)
Async XLA Ops:
  6.5 6.5 copy-start.1
  6.5 7.0 copy-start.2
  6.5 190.5 %all-to-all-start = ((bf16[8,4096,128]{2,1,0:T(8,128)(2,1)}), bf16[8,4096,128]{2,1,0:T(8,128)(2,1)}, u32[]{:S(2)}, u32[]{:S(2)}) async-start(bf16[8,4096,128]{2,1,0:T(8,128)(2,1)} %bitcast.180), calls=%async_computation | async-start | bytes 16777216 | tf_op jit(solution)/shard_map/all_to_all | solution.py:76
  13.0 546.4 %all-reduce.6.cloned.1.call-start = ((), (), s32[]{:S(2)}) async-start(), calls=%async_computation.3 | async-start | bytes 9437184
  445.8 5.6 copy-start
  449.2 4.8 copy-start.4
  449.2 5.5 copy-start.3
  454.0 154.6 %all-reduce.4.cloned.1.call-start = ((), (), s32[]{:S(2)}) async-start(), calls=%async_computation.2 | async-start | bytes 1179648 | tf_op jit(solution)/shard_map/psum | solution.py:92
Sparse Core Ops, SparseCore 0:
  454.1 105.2 all-reduce.5
  562.4 46.1 all-reduce.3
where the time goes:
time: 994 us; the launch traced here: 982 us
  waiting for transfers between devices  325 us (33%)
  local copies, waits for them, and re-layouts  314 us (32%)
  blocking collectives  205 us (21%)
  matrix products  86.3 us (9%)
  other arithmetic  30.6 us (3%)
  between operations  15.1 us (2%)
    all_to_all x1, blocking collectives, body(): lax.all_to_all(local_rows, 'orb', split_axis=1, concat_axis=0, tiled=True)  190 us
    all_to_all x1, waiting for transfers between devices, body(): lax.all_to_all(coeffs, 'orb', split_axis=0, concat_axis=1, tiled=True)  183 us
    unnamed x3, waiting for transfers between devices  105 us
    transpose x3, local copies, waits for them, and re-layouts, jacobi_pair(): jnp.einsum('ji,kjl->kil', rotation, jnp.einsum('kij,jl->kil', gram, rotat...  50.4 us
    gather x3, local copies, waits for them, and re-layouts, gram_terms(): moment_blocks[:, :, partner]  39.6 us
    psum x1, waiting for transfers between devices, body(): summed = lax.psum(summed, 'bas')  37 us
    convert_element_type x1, local copies, waits for them, and re-layouts, project_rows(): moments = jnp.einsum('kraj,rjn->kran', dipole_rows, picked, preferred_ele...  32.6 us
    reshape x1, local copies, waits for them, and re-layouts, project_rows(): return moments.reshape(3, group_tiles * TILE, blocks, BLK)  31.7 us
  transfers between devices with their start and end apart: 3, of which 3 were waited for; matrix products, arithmetic and copies ran while one was open for 1% of the time, Pallas kernels for 0%

commit v1 on v0

--- a/solution.py
+++ b/solution.py
@@ -89,7 +89,7 @@
     my_leader = leader[my_block]
     entries = jnp.stack([self_gram[leader], self_gram[follower], cross_gram], axis=1)
     summed = lax.psum_scatter(entries, "orb", scatter_dimension=0, tiled=True)[0]
-    summed = lax.psum(summed, "bas")
+    summed = jnp.sum(lax.all_gather(summed, "bas"), axis=0)
     lead_gram = summed[0]
     follow_gram = summed[1]
     cross_mine = summed[2]

time: 994 us -> 986 us (level)
    psum x1 -> x0, waiting for transfers between devices: 37 us -> none  [body(): summed = lax.psum(summed, 'bas')]
    all_gather x0 -> x1, waiting for transfers between devices: none -> 28 us  [body(): summed = jnp.sum(lax.all_gather(summed, 'bas'), axis=0)]
    unnamed x15 -> x16, local copies, waits for them, and re-layouts: 24.2 us -> 26.8 us
where the time goes in v1:
time: 986 us; the launch traced here: 974 us
  waiting for transfers between devices  316 us (32%)
  local copies, waits for them, and re-layouts  313 us (32%)
  blocking collectives  205 us (21%)
  matrix products  86.3 us (9%)
  other arithmetic  32.4 us (3%)
  between operations  15.1 us (2%)
    all_to_all x1, blocking collectives, body(): lax.all_to_all(local_rows, 'orb', split_axis=1, concat_axis=0, tiled=True)  190 us
    all_to_all x1, waiting for transfers between devices, body(): lax.all_to_all(coeffs, 'orb', split_axis=0, concat_axis=1, tiled=True)  183 us
    unnamed x3, waiting for transfers between devices  105 us
    transpose x3, local copies, waits for them, and re-layouts, jacobi_pair(): jnp.einsum('ji,kjl->kil', rotation, jnp.einsum('kij,jl->kil', gram, rotat...  50.4 us
    gather x3, local copies, waits for them, and re-layouts, gram_terms(): moment_blocks[:, :, partner]  39.6 us
    convert_element_type x1, local copies, waits for them, and re-layouts, project_rows(): moments = jnp.einsum('kraj,rjn->kran', dipole_rows, picked, preferred_ele...  32.6 us
    reshape x1, local copies, waits for them, and re-layouts, project_rows(): return moments.reshape(3, group_tiles * TILE, blocks, BLK)  31.7 us
    all_gather x1, waiting for transfers between devices, body(): summed = jnp.sum(lax.all_gather(summed, 'bas'), axis=0)  28 us
  transfers between devices with their start and end apart: 3, of which 3 were waited for; matrix products, arithmetic and copies ran while one was open for 1% of the time, Pallas kernels for 0%

profile of v1, /device:TPU:0, one launch (start us, length us, event | category | flops | bytes accessed | tf_op | source)
XLA Modules:
  0.0 974.2 jit_solution(9588552163212918512)
XLA Ops:
  14.1 182.9 %all-to-all-done = bf16[8,4096,128]{2,1,0:T(8,128)(2,1)} async-done(((bf16[8,4096,128]{2,1,0:T(8,128)(2,1)}), bf16[8,4096,128]{2,1,0:T(8,128)(2,1)}, u32[]{:S(2)}, u32[]{:S(2)}) %all-to-all-start) | async-done | bytes 8388640 | tf_op jit(solution)/shard_map/all_to_all | solution.py:76
  207.3 13.3 %reshape.298 = bf16[32,128,1024]{2,1,0:T(8,128)(2,1)} reshape(bf16[4096,8,128]{2,1,0:T(8,128)(2,1)} %copy.135) | data formatting | bytes 16777216 | tf_op jit(solution)/shard_map/reshape | solution.py:50
  220.6 13.6 %gather_fusion = bf16[96,128,1024]{2,1,0:T(8,128)(2,1)} fusion(bf16[32,128,1024]{2,1,0:T(8,128)(2,1)} %reshape.298, s32[1024]{0:T(1024)S(1)} %pad_clamp_fusion.3), kind=kCustom, calls=%fused_computation | custom fusion | bytes 50332032 | tf_op jit(solution)/shard_map/gather | solution.py:51
  234.2 20.9 %bitcast_select_fusion = bf16[32,384,1024]{2,1,0:T(8,128)(2,1)} fusion(pred[32,384]{1,0:T(8,128)(4,1)S(1)} %bitcast.183, bf16[32,384,1024]{2,1,0:T(8,128)(2,1)} %bitcast.174), kind=kLoop, calls=%fused_computation.22 | loop fusion | flops 12582912 | bytes 50343936 | tf_op jit(solution)/shard_map/jit(_where)/select_n | solution.py:52
  255.1 25.8 %convert_bitcast_fusion = bf16[3,32,128,1024]{2,3,0,1:T(8,128)(2,1)} fusion(bf16[32,384,1024]{2,1,0:T(8,128)(2,1)} %bitcast_select_fusion, bf16[3,32,128,384]{3,2,1,0:T(8,128)(2,1)} %bitcast.198), kind=kOutput, calls=%fused_computation.23 | convolution fusion | flops 9676259328 | bytes 59768832 | tf_op jit(solution)/shard_map/kraj,rjn->kran/dot_general | solution.py:54
  281.0 32.6 %copy.139 = bf16[3,32,128,1024]{3,2,1,0:T(8,128)(2,1)} copy(bf16[3,32,128,1024]{2,3,0,1:T(8,128)(2,1)} %convert_bitcast_fusion) | data formatting | bytes 50331648 | tf_op jit(solution)/shard_map/convert_element_type | solution.py:56
  313.5 23.2 %copy.185 = bf16[1536,8,8,128]{3,2,1,0:T(8,128)(2,1)} copy(bf16[1536,8,8,128]{3,1,2,0:T(8,128)(2,1)} %bitcast.172) | data formatting | bytes 50331648
  336.7 31.7 %copy.140 = bf16[3,4096,8,128]{1,3,0,2:T(8,128)(2,1)} copy(bf16[3,4096,8,128]{3,2,1,0:T(8,128)(2,1)} %bitcast.173) | data formatting | bytes 50331648 | tf_op jit(solution)/shard_map/reshape | solution.py:57
  368.4 17.8 %fusion.95 = (bf16[3,2048,8,128]{1,3,0,2:T(8,128)(2,1)}, bf16[3,2048,8,128]{1,3,0,2:T(8,128)(2,1)}) fusion(bf16[3,4096,8,128]{1,3,0,2:T(8,128)(2,1)} %copy.140), kind=kLoop, calls=%fused_computation.191 | loop fusion | bytes 50331648 | tf_op jit(solution)/shard_map/gather | solution.py:68
  386.2 10.9 %gather_fusion.14 = bf16[8,3,2048,128]{2,3,1,0:T(8,128)(2,1)} fusion(bf16[3,2048,8,128]{1,3,0,2:T(8,128)(2,1)} %get-tuple-element.21, s32[1024]{0:T(1024)S(1)} %get-tuple-element.40), kind=kCustom, calls=%fused_computation.14 | custom fusion | bytes 25165856 | tf_op jit(solution)/shard_map/gather | solution.py:68
  397.1 10.9 %gather_fusion.15 = bf16[8,3,2048,128]{2,3,1,0:T(8,128)(2,1)} fusion(bf16[3,2048,8,128]{1,3,0,2:T(8,128)(2,1)} %get-tuple-element.22, s32[1024]{0:T(1024)S(1)} %get-tuple-element.40), kind=kCustom, calls=%fused_computation.15 | custom fusion | bytes 25165856 | tf_op jit(solution)/shard_map/gather | solution.py:68
  408.0 14.5 %fusion.19 = f32[8,3,128,128]{2,3,1,0:T(8,128)S(1)} fusion(bf16[8,4096,128]{2,1,0:T(8,128)(2,1)} %all-to-all-done, bf16[3,2048,8,128]{1,3,0,2:T(8,128)(2,1)} %bitcast.177, bf16[3,2048,8,128]{1,3,0,2:T(8,128)(2,1)} %bitcast.176), kind=kOutput, calls=%fused_computation.37 | convolution fusion | flops 3271557120 | bytes 35127296 | tf_op jit(solution)/shard_map/rbi,krbj->bkij/dot_general | solution.py:65
  426.0 14.0 %fusion.11 = f32[8,3,128,128]{3,2,1,0:T(8,128)S(1)} fusion(bf16[3,4096,8,128]{1,3,0,2:T(8,128)(2,1)} %copy.140, bf16[8,4096,128]{2,1,0:T(8,128)(2,1)} %all-to-all-done), kind=kOutput, calls=%fused_computation.28 | convolution fusion | flops 3221225472 | bytes 35127296 | tf_op jit(solution)/shard_map/rbi,krbj->bkij/dot_general | solution.py:61
  454.7 104.7 %all-reduce.3.cloned.1.call-done = f32[8,3,3,128,128]{4,3,2,0,1:T(8,128)} async-done(((f32[8,3,3,128,128]{4,3,2,0,1:T(8,128)}), f32[8,3,3,128,128]{4,3,2,0,1:T(8,128)}) %all-reduce.3.cloned.1.call-update) | async-done | bytes 4718608
  571.7 28.0 %all-gather.3.cloned.1.call-done = f32[4,3,3,128,128]{4,3,2,0,1:T(8,128)} async-done(((f32[1,3,3,128,128]{4,3,2,0,1:T(8,128)}), f32[4,3,3,128,128]{4,3,2,0,1:T(8,128)}) %all-gather.3.cloned.1.call-update) | async-done | bytes 2359312 | tf_op jit(solution)/shard_map/all_gather | solution.py:92
  608.4 16.9 %copy.148 = f32[3,256,256]{0,2,1:T(8,128)} copy(f32[3,256,256]{2,1,0:T(8,128)S(1)} %maximum_maximum_fusion) | data formatting | bytes 1572864 | tf_op jit(solution)/shard_map/concatenate | solution.py:98
  630.1 16.7 %copy.153 = f32[3,256,256]{0,2,1:T(8,128)} copy(f32[3,256,256]{1,2,0:T(8,128)S(1)} %convolution_bitcast_fusion.2) | data formatting | bytes 1572864 | tf_op jit(solution)/shard_map/ji,kjl->kil/transpose | solution.py:38
  662.3 16.9 %copy.159 = f32[3,256,256]{0,2,1:T(8,128)} copy(f32[3,256,256]{1,2,0:T(8,128)S(1)} %convolution_bitcast_fusion.1) | data formatting | bytes 1572864 | tf_op jit(solution)/shard_map/ji,kjl->kil/transpose | solution.py:38
  693.6 16.7 %copy.165 = f32[3,256,256]{0,2,1:T(8,128)} copy(f32[3,256,256]{1,2,0:T(8,128)S(1)} %convolution_bitcast_fusion) | data formatting | bytes 1572864 | tf_op jit(solution)/shard_map/ji,kjl->kil/transpose | solution.py:38
  724.2 15.0 %all-gather = bf16[2048,128]{1,0:T(8,128)(2,1)S(1)} all-gather(bf16[256,128]{1,0:T(8,128)(2,1)S(1)} %fusion.47), channel_id=2, replica_groups=mesh['orb'=8,'bas'=4] {'orb'}, dimensions={0}, use_global_device_ids=true | all-gather | bytes 589824 | tf_op jit(solution)/shard_map/all_gather | solution.py:100
  739.6 11.5 %fusion.42 = f32[8,128,4096]{2,1,0:T(8,128)} fusion(bf16[8,128,128]{1,2,0:T(8,128)(2,1)S(1)} %copy.182, bf16[8,128,128]{1,2,0:T(8,128)(2,1)S(1)} %copy.183, pred[8]{0:T(512)(128)(4,1)S(1)} %iota_compare_fusion.11, bf16[8,4096,128]{2,1,0:T(8,128)(2,1)} %all-to-all-done), kind=kOutput, calls=%fused_computation.63 | convolution fusion | flops 1073872896 | bytes 25690120 | tf_op jit(solution)/shard_map/rbj,bjn->rbn/dot_general | solution.py:104
  751.1 14.0 %fusion.13 = bf16[4096,8,128]{0,2,1:T(8,128)(2,1)} fusion(f32[8,128,4096]{2,1,0:T(8,128)} %fusion.42, bf16[8,4096,128]{2,1,0:T(8,128)(2,1)} %gather_fusion.13, bf16[8,128,128]{1,2,0:T(8,128)(2,1)S(1)} %copy.183, bf16[8,128,128]{1,2,0:T(8,128)(2,1)S(1)} %copy.182, pred[8]{0:T(512)(128)(4,1)S(1)} %iota_compare_fusion.11), kind=kOutput, calls=%fused_computation.30 | convolution fusion | flops 1082261504 | bytes 34078728 | tf_op jit(solution)/shard_map/rbj,bjn->rbn/dot_general | solution.py:107
  765.1 189.9 %all_to_all.32 = bf16[4096,8,128]{0,2,1:T(8,128)(2,1)} all-to-all(bf16[4096,8,128]{0,2,1:T(8,128)(2,1)} %fusion.13), channel_id=1, replica_groups=mesh['orb'=8,'bas'=4] {'orb'}, dimensions={1} | all-to-all | bytes 16777216 | tf_op jit(solution)/shard_map/all_to_all | solution.py:111
  955.0 11.9 %copy.169 = bf16[8,4096,128]{2,1,0:T(8,128)(2,1)} copy(bf16[8,4096,128]{1,2,0:T(8,128)(2,1)} %bitcast.175) | data formatting | bytes 16777216 | tf_op jit(solution)/shard_map/all_to_all | solution.py:111
  (130 shorter events, 104.8 us)
Async XLA Ops:
  6.5 6.5 copy-start.1
  6.5 7.0 copy-start.2
  6.5 190.5 %all-to-all-start = ((bf16[8,4096,128]{2,1,0:T(8,128)(2,1)}), bf16[8,4096,128]{2,1,0:T(8,128)(2,1)}, u32[]{:S(2)}, u32[]{:S(2)}) async-start(bf16[8,4096,128]{2,1,0:T(8,128)(2,1)} %bitcast.178), calls=%async_computation | async-start | bytes 16777216 | tf_op jit(solution)/shard_map/all_to_all | solution.py:76
  13.0 546.4 %all-reduce.3.cloned.1.call-start = ((), (), s32[]{:S(2)}) async-start(), calls=%async_computation.3 | async-start | bytes 9437184
  445.8 5.6 copy-start
  449.2 4.8 copy-start.4
  451.4 110.7 %copy-start.3 = (s32[1,8]{1,0:T(1,128)S(1)}, s32[1,8]{1,0:T(1,128)}, u32[]{:S(2)}) copy-start(s32[1,8]{1,0:T(1,128)} %param.7) | copy-start | bytes 100
  454.0 145.7 %all-gather.3.cloned.1.call-start = ((), (), s32[]{:S(2)}) async-start(), calls=%async_computation.2 | async-start | bytes 2949120 | tf_op jit(solution)/shard_map/all_gather | solution.py:92
Sparse Core Ops, SparseCore 0:
  454.1 105.2 all-reduce.2
  562.1 37.5 all-gather.2
